TPU v7x, 32 devices: a whole 2x2x4 slice. The times are simulated.
32 devices in a mesh: groups: 2 (over y), row: 4 (over x, core), col: 4 (over z).
Axes of the slice: x: 2, y: 2, z: 4, core: 2. Of those that a mesh axis runs over, the one named last changes fastest.
Arguments:
- pair_norm: bfloat16 [256, 128, 128], P(('groups', 'row'), 'col'), parts along dimension 0, may hold values from -5 to 5
- pair_rstd: float32 [256, 128], P(('groups', 'row'), 'col'), parts along dimension 0, may hold values from 0.3 to 3
- out_norm: bfloat16 [256, 128, 128], P(('groups', 'row'), 'col'), parts along dimension 0, may hold values from -5 to 5
- out_rstd: float32 [256, 128], P(('groups', 'row'), 'col'), parts along dimension 0, may hold values from 0.3 to 3
- grad_out: bfloat16 [256, 128, 128], P(('groups', 'row'), 'col'), parts along dimension 0, may hold values from -6 to 6
- token_mask: int32 [256], P('groups'), parts along dimension 0, may hold values 0 or 1
- proj_weight: bfloat16 [128, 512], replicated, may hold values from -0.5 to 0.5
- gate_weight: bfloat16 [128, 128], replicated, may hold values from -0.5 to 0.5
- out_weight: bfloat16 [128, 128], replicated, may hold values from -0.5 to 0.5
- out_gain: float32 [128], replicated, may hold values from 0.1 to 1.9
- out_bias: float32 [128], replicated, may hold values from -3 to 3
Outputs:
- pair_grad: float32 [256, 128, 128], P(('groups', 'row'), 'col'), parts along dimension 0
- proj_wgrad: float32 [256, 512], P('groups'), parts along dimension 0
- gate_wgrad: float32 [256, 128], P('groups'), parts along dimension 0
There are 2 independent parts, one for each index of `groups`. A program takes and returns all parts, laid end to end along the dimension named above; an argument that names none is the same for every part. Nothing has to cross between parts.
All inputs are finite; a program needn't handle non-finite values.
Results may differ from a plain program's by a relative error of at most 0.008.
Values may be sent and summed in bfloat16 or wider, within the bound.
A program may use at most 128 MiB of HBM per device.

v0:
```python
import jax
import jax.numpy as jnp
from jax import lax
from jax.sharding import PartitionSpec as P


def spread(x, axis, root):
    mine = lax.axis_index(axis) == root
    return lax.psum(jnp.where(mine, x, jnp.zeros_like(x)), axis)


def local(
    pair_norm,
    pair_rstd,
    out_norm,
    out_rstd,
    grad_out,
    token_mask,
    proj_weight,
    gate_weight,
    out_weight,
    out_gain,
    out_bias,
):
    f32 = jnp.float32
    tile_rows, tile_cols, width = pair_norm.shape
    hidden = out_weight.shape[0]
    cells = tile_rows * tile_cols
    col_ratio = lax.axis_size("col") // lax.axis_size("row")
    row_at = lax.axis_index("row")
    col_at = lax.axis_index("col")
    mask_vals = token_mask.astype(f32)
    mask_rows = lax.dynamic_slice_in_dim(mask_vals, row_at * tile_rows, tile_rows)
    mask_cols = lax.dynamic_slice_in_dim(mask_vals, col_at * tile_cols, tile_cols)
    pair_mask = (mask_rows[:, None] * mask_cols[None, :])[:, :, None]
    flat_norm = pair_norm.reshape(cells, width)
    projected = jnp.dot(flat_norm, proj_weight, preferred_element_type=f32).reshape(
        tile_rows, tile_cols, 4 * hidden
    )
    left_gate = jax.nn.sigmoid(projected[..., :hidden])
    left_value = projected[..., hidden : 2 * hidden]
    right_gate = jax.nn.sigmoid(projected[..., 2 * hidden : 3 * hidden])
    right_value = projected[..., 3 * hidden :]
    left_proj = (pair_mask * left_gate * left_value).astype(jnp.bfloat16)
    right_proj = (pair_mask * right_gate * right_value).astype(jnp.bfloat16)
    gate_sig = jax.nn.sigmoid(jnp.dot(flat_norm, gate_weight, preferred_element_type=f32))
    hat_out = out_norm.reshape(cells, hidden).astype(f32)
    normed_out = (hat_out * out_gain + out_bias).astype(jnp.bfloat16)
    update = jnp.dot(normed_out, out_weight, preferred_element_type=f32)
    upstream = grad_out.reshape(cells, width).astype(f32)
    gate_grad = (upstream * update * gate_sig * (1.0 - gate_sig)).astype(jnp.bfloat16)
    update_grad = (upstream * gate_sig).astype(jnp.bfloat16)
    gate_part = lax.dot_general(
        flat_norm, gate_grad, (((0,), (0,)), ((), ())), preferred_element_type=f32
    )
    normed_grad = (
        lax.dot_general(
            update_grad, out_weight, (((1,), (1,)), ((), ())), preferred_element_type=f32
        )
        * out_gain
    )
    tri_grad = out_rstd.reshape(cells, 1) * (
        normed_grad
        - jnp.mean(normed_grad, axis=-1, keepdims=True)
        - hat_out * jnp.mean(normed_grad * hat_out, axis=-1, keepdims=True)
    )
    tri_grad = tri_grad.astype(jnp.bfloat16).reshape(tile_rows, tile_cols, hidden)
    left_cols, right_cols = (
        lax.all_gather(left_proj, "row", axis=0, tiled=True),
        lax.all_gather(right_proj, "row", axis=0, tiled=True),
    )
    left_total = lax.dot_general(
        lax.all_gather(tri_grad, "col", axis=1, tiled=True),
        right_cols,
        (((1,), (0,)), ((2,), (2,))),
        preferred_element_type=f32,
    )
    grad_cols = lax.all_gather(tri_grad, "row", axis=0, tiled=True)
    blocks = []
    for offset in range(col_ratio):
        panel = spread(grad_cols, "col", row_at * col_ratio + offset)
        blocks.append(
            lax.dot_general(
                panel, left_cols, (((0,), (0,)), ((2,), (2,))), preferred_element_type=f32
            )
        )
    right_turned = jnp.concatenate(blocks, axis=1)
    left_grad = jnp.transpose(left_total, (1, 2, 0))
    right_grad = jnp.transpose(right_turned, (1, 2, 0))
    proj_grad = (
        jnp.concatenate(
            [
                left_grad * pair_mask * left_value * left_gate * (1.0 - left_gate),
                left_grad * pair_mask * left_gate,
                right_grad * pair_mask * right_value * right_gate * (1.0 - right_gate),
                right_grad * pair_mask * right_gate,
            ],
            axis=-1,
        )
        .astype(jnp.bfloat16)
        .reshape(cells, 4 * hidden)
    )
    proj_part = lax.dot_general(
        flat_norm, proj_grad, (((0,), (0,)), ((), ())), preferred_element_type=f32
    )
    proj_wgrad, gate_wgrad = lax.psum((proj_part, gate_part), ("row", "col"))
    norm_grad = lax.dot_general(
        gate_grad, gate_weight, (((1,), (1,)), ((), ())), preferred_element_type=f32
    ) + lax.dot_general(
        proj_grad, proj_weight, (((1,), (1,)), ((), ())), preferred_element_type=f32
    )
    pair_vals = flat_norm.astype(f32)
    pair_grad = pair_rstd.reshape(cells, 1) * (
        norm_grad
        - jnp.mean(norm_grad, axis=-1, keepdims=True)
        - pair_vals * jnp.mean(norm_grad * pair_vals, axis=-1, keepdims=True)
    )
    return (pair_grad.reshape(tile_rows, tile_cols, width), proj_wgrad, gate_wgrad)


def solution(mesh):
    placed = (
        P(("groups", "row"), "col", None),
        P(("groups", "row"), "col"),
        P(("groups", "row"), "col", None),
        P(("groups", "row"), "col"),
        P(("groups", "row"), "col", None),
        P("groups"),
        P(),
        P(),
        P(),
        P(),
        P(),
    )
    return jax.shard_map(
        local,
        mesh=mesh,
        in_specs=placed,
        out_specs=(P(("groups", "row"), "col", None), P("groups", None), P("groups", None)),
        check_vma=False,
    )
```

profile of v0, /device:TPU:0, one launch (start us, length us, event | category | flops | bytes accessed | tf_op | source)
XLA Modules:
  0.0 261.0 jit_solution(6593507764352822410)
XLA Ops:
  7.2 0.0 all-gather.9.cloned.1.call-start
  7.3 0.9 mul.170
  8.1 1.3 fusion.2
  9.5 0.5 fusion.53
  10.0 1.2 fusion.29
  11.2 0.0 all-gather.7.cloned.1.call-start
  11.3 0.1 fusion.54
  11.4 0.1 broadcast_multiply_fusion
  11.5 0.4 fusion.48
  11.9 1.1 multiply_convert_fusion.1
  13.0 0.0 all-gather.7.cloned.1.call-update
  13.0 0.0 all-gather.5.cloned.1.call-start
  13.1 0.8 copy.22
  13.9 0.0 all-gather.11.cloned.1.call-start
  14.0 0.5 all-gather.11.cloned.1.call-update
  14.5 0.0 all-reduce.4.cloned.1.call-start
  14.6 0.7 mul.163
  15.2 15.6 %all-gather.9.cloned.1.call-done = bf16[128,32,128]{2,1,0:T(8,128)(2,1)} async-done(((bf16[32,32,128]{2,1,0:T(8,128)(2,1)}), bf16[128,32,128]{2,1,0:T(8,128)(2,1)}) %all-gather.9.cloned.1.call-update) | async-done | bytes 1048592 | tf_op jit(solution)/shard_map/all_gather | solution.py:78
  30.8 2.5 copy.26
  33.3 1.2 broadcast_select_fusion
  34.5 0.0 all-reduce.4.cloned.1.call-update
  34.5 0.2 all-reduce.6.cloned.1.call-start
  34.7 1.5 fusion.5
  36.2 0.9 convolution_bitcast_fusion.1
  37.1 1.0 fusion.55
  38.1 11.0 %all-gather.7.cloned.1.call-done = bf16[128,32,128]{2,1,0:T(8,128)(2,1)} async-done(((bf16[32,32,128]{2,1,0:T(8,128)(2,1)}), bf16[128,32,128]{2,1,0:T(8,128)(2,1)}) %all-gather.7.cloned.1.call-update) | async-done | bytes 1048592 | tf_op jit(solution)/shard_map/all_gather | solution.py:70
  49.2 7.2 %copy.24 = bf16[128,32,128]{1,0,2:T(8,128)(2,1)} copy(bf16[128,32,128]{2,1,0:T(8,128)(2,1)} %all-gather.7.cloned.1.call-done) | data formatting | bytes 2097152 | tf_op jit(solution)/shard_map/all_gather | solution.py:70
  56.4 22.3 %all-gather.5.cloned.1.call-done = bf16[32,128,128]{2,0,1:T(8,128)(2,1)} async-done(((bf16[32,32,128]{2,0,1:T(8,128)(2,1)}), bf16[32,128,128]{2,0,1:T(8,128)(2,1)}) %all-gather.5.cloned.1.call-update) | async-done | bytes 1048592 | tf_op jit(solution)/shard_map/all_gather | solution.py:73
  78.7 2.5 copy.23
  81.2 4.7 %fusion.56 = f32[128,32,32]{2,1,0:T(8,128)} fusion(bf16[32,128,128]{1,0,2:T(8,128)(2,1)S(1)} %copy.23, bf16[128,32,128]{1,0,2:T(8,128)(2,1)} %copy.24), kind=kOutput, calls=%fused_computation.80 | convolution fusion | flops 33554432 | bytes 2621440 | tf_op jit(solution)/shard_map/dot_general | solution.py:72
  85.9 2.8 %copy.25 = f32[128,32,32]{0,2,1:T(8,128)S(1)} copy(f32[128,32,32]{2,1,0:T(8,128)} %fusion.56) | data formatting | bytes 1048576 | tf_op jit(solution)/shard_map/dot_general | solution.py:72
  88.7 7.7 %all-gather.11.cloned.1.call-done = bf16[128,32,128]{2,1,0:T(8,128)(2,1)} async-done(((bf16[32,32,128]{2,1,0:T(8,128)(2,1)}), bf16[128,32,128]{2,1,0:T(8,128)(2,1)}) %all-gather.11.cloned.1.call-update) | async-done | bytes 1048592 | tf_op jit(solution)/shard_map/all_gather | solution.py:69
  96.4 7.2 %copy.27 = bf16[128,32,128]{1,0,2:T(8,128)(2,1)} copy(bf16[128,32,128]{2,1,0:T(8,128)(2,1)} %all-gather.11.cloned.1.call-done) | data formatting | bytes 2097152 | tf_op jit(solution)/shard_map/all_gather | solution.py:69
  103.6 46.8 %all-reduce.4.cloned.1.call-done = bf16[128,32,128]{0,1,2:T(8,128)(2,1)} async-done(((bf16[128,32,128]{0,1,2:T(8,128)(2,1)}), bf16[128,32,128]{0,1,2:T(8,128)(2,1)}) %all-reduce.4.cloned.1.call-update) | async-done | bytes 1048592 | tf_op jit(solution)/shard_map/psum | solution.py:9
  150.4 5.1 %fusion.57 = f32[128,32,32]{2,1,0:T(8,128)} fusion(bf16[128,32,128]{0,1,2:T(8,128)(2,1)} %all-reduce.4.cloned.1.call-done, bf16[128,32,128]{1,0,2:T(8,128)(2,1)} %copy.27), kind=kOutput, calls=%fused_computation.81 | convolution fusion | flops 33554432 | bytes 2621440 | tf_op jit(solution)/shard_map/dot_general | solution.py:83
  155.5 2.7 %copy.28 = f32[128,32,32]{0,2,1:T(8,128)S(1)} copy(f32[128,32,32]{2,1,0:T(8,128)} %fusion.57) | data formatting | bytes 1048576 | tf_op jit(solution)/shard_map/dot_general | solution.py:83
  158.1 0.5 fusion.42
  158.7 0.7 copy-done.7
  159.3 0.1 copy-done.8
  159.4 0.1 copy-done.9
  159.5 0.1 copy-done.10
  159.6 1.2 convolution_bitcast_fusion
  160.8 1.7 fusion.52
  162.5 0.0 all-reduce.6.cloned.1.call-update
  162.6 1.3 fusion.22
  163.8 86.9 %all-reduce.6.cloned.1.call-done = (f32[128,512]{0,1:T(8,128)}, f32[128,128]{0,1:T(8,128)}) async-done(((f32[128,512]{0,1:T(8,128)}, f32[128,128]{0,1:T(8,128)}), (f32[128,512]{0,1:T(8,128)}, f32[128,128]{0,1:T(8,128)})) %all-reduce.6.cloned.1.call-update) | async-done | bytes 327696 | tf_op jit(solution)/shard_map/psum | solution.py:106
  250.8 1.8 copy.29
  252.6 1.6 copy.30
  (36 shorter events, 0.1 us)
Async XLA Ops:
  7.2 4.3 %copy-start = (bf16[128,512]{1,0:T(8,128)(2,1)S(1)}, bf16[128,512]{1,0:T(8,128)(2,1)}, u32[]{:S(2)}) copy-start(bf16[128,512]{1,0:T(8,128)(2,1)} %param.17) | copy-start | bytes 393220
  7.2 2.3 copy-start.5
  7.2 2.3 copy-start.3
  7.2 2.3 copy-start.11
  7.2 2.3 copy-start.15
  7.2 23.6 %all-gather.9.cloned.1.call-start = ((), (), s32[]{:S(2)}) async-start(), calls=%async_computation.2 | async-start | bytes 1310720 | tf_op jit(solution)/shard_map/all_gather | solution.py:78
  8.1 3.2 %copy-start.16 = (s32[128]{0:T(128)S(1)}, s32[128]{0:T(128)}, u32[]{:S(2)}) copy-start(s32[128]{0:T(128)} %param.16) | copy-start | bytes 1540
  8.1 3.4 %copy-start.1 = (bf16[32,32,128]{2,1,0:T(8,128)(2,1)S(1)}, bf16[32,32,128]{2,1,0:T(8,128)(2,1)}, u32[]{:S(2)}) copy-start(bf16[32,32,128]{2,1,0:T(8,128)(2,1)} %param.11) | copy-start | bytes 786436
  9.4 2.0 copy-start.4
  11.2 37.9 %all-gather.7.cloned.1.call-start = ((), (), s32[]{:S(2)}) async-start(), calls=%async_computation.1 | async-start | bytes 1310720 | tf_op jit(solution)/shard_map/all_gather | solution.py:70
  11.5 1.6 copy-start.2
  11.9 2.7 %copy-start.14 = (f32[32,32]{1,0:T(8,128)S(1)}, f32[32,32]{1,0:T(8,128)}, u32[]{:S(2)}) copy-start(f32[32,32]{1,0:T(8,128)} %param.12) | copy-start | bytes 12292
  13.0 65.6 %all-gather.5.cloned.1.call-start = ((), (), s32[]{:S(2)}) async-start(), calls=%async_computation | async-start | bytes 1310720 | tf_op jit(solution)/shard_map/all_gather | solution.py:73
  13.9 82.4 %all-gather.11.cloned.1.call-start = ((), (), s32[]{:S(2)}) async-start(), calls=%async_computation.4 | async-start | bytes 1310720 | tf_op jit(solution)/shard_map/all_gather | solution.py:69
  14.5 135.9 %all-reduce.4.cloned.1.call-start = ((), (), s32[]{:S(2)}) async-start(), calls=%async_computation.3 | async-start | bytes 2097152 | tf_op jit(solution)/shard_map/psum | solution.py:9
  34.5 2.7 %copy-start.12 = (bf16[128,128]{1,0:T(8,128)(2,1)S(1)}, bf16[128,128]{1,0:T(8,128)(2,1)}, u32[]{:S(2)}) copy-start(bf16[128,128]{1,0:T(8,128)(2,1)} %param.18) | copy-start | bytes 98308
  34.5 216.3 %all-reduce.6.cloned.1.call-start = ((), (), s32[]{:S(2)}) async-start(), calls=%async_computation.5 | async-start | bytes 655360 | tf_op jit(solution)/shard_map/psum | solution.py:106
  158.6 0.7 copy-start.7
  158.6 0.8 copy-start.8
  158.6 0.9 copy-start.9
  158.7 0.9 copy-start.10
  159.6 1.2 copy-start.6
  160.8 1.8 copy-start.13
Sparse Core Ops, SparseCore 0:
  11.4 19.4 all-gather.8
  32.4 16.7 all-gather.6
  50.7 27.9 all-gather.4
  80.1 16.2 all-gather.10
  98.6 51.8 all-reduce.3
  162.7 88.0 all-reduce.5
where the time goes:
time: 262 us; the launch traced here: 261 us
  waiting for transfers between devices  191 us (73%)
  local copies, waits for them, and re-layouts  31.6 us (12%)
  matrix products  18.4 us (7%)
  between operations  14.4 us (5%)
  other arithmetic  5.29 us (2%)
    psum x1, waiting for transfers between devices, local(): proj_wgrad, gate_wgrad = lax.psum((proj_part, gate_part), ('row', 'col'))  86.9 us
    psum x1, waiting for transfers between devices, spread(): return lax.psum(jnp.where(mine, x, jnp.zeros_like(x)), axis)  46.8 us
    all_gather x1, waiting for transfers between devices, local(): lax.all_gather(tri_grad, 'col', axis=1, tiled=True)  22.3 us
    all_gather x1, waiting for transfers between devices, local(): grad_cols = lax.all_gather(tri_grad, 'row', axis=0, tiled=True)  15.6 us
    all_gather x1, waiting for transfers between devices, local(): lax.all_gather(right_proj, 'row', axis=0, tiled=True)  11 us
    all_gather x1, waiting for transfers between devices, local(): lax.all_gather(left_proj, 'row', axis=0, tiled=True)  7.68 us
    all_gather x1, local copies, waits for them, and re-layouts, local(): lax.all_gather(right_proj, 'row', axis=0, tiled=True)  7.23 us
    all_gather x1, local copies, waits for them, and re-layouts, local(): lax.all_gather(left_proj, 'row', axis=0, tiled=True)  7.23 us
  transfers between devices with their start and end apart: 6, of which 6 were waited for; matrix products, arithmetic and copies ran while one was open for 14% of the time, Pallas kernels for 0%

commit v1 on v0

--- a/solution.py
+++ b/solution.py
@@ -1,6 +1,10 @@
+import functools
+
 import jax
 import jax.numpy as jnp
 from jax import lax
+from jax.experimental import pallas as pl
+from jax.experimental.pallas import tpu as pltpu
 from jax.sharding import PartitionSpec as P
 
 
@@ -9,7 +13,7 @@
     return lax.psum(jnp.where(mine, x, jnp.zeros_like(x)), axis)
 
 
-def local(
+def plain(
     pair_norm,
     pair_rstd,
     out_norm,
@@ -118,6 +122,477 @@
     return (pair_grad.reshape(tile_rows, tile_cols, width), proj_wgrad, gate_wgrad)
 
 
+F32 = jnp.float32
+BF16 = jnp.bfloat16
+MESH = pl.DeviceIdType.MESH
+ROWS_DOT = (((0,), (0,)), ((), ()))
+LANES_DOT = (((1,), (1,)), ((), ()))
+GROUP = 4
+
+
+def kernel(
+    side,
+    tile,
+    x_ref,
+    pair_rstd_ref,
+    hat_ref,
+    out_rstd_ref,
+    up_ref,
+    mask_ref,
+    proj_ref,
+    gate_ref,
+    out_ref,
+    gain_ref,
+    bias_ref,
+    pair_out,
+    proj_out,
+    gate_out,
+    tri_all,
+    right_all,
+    part_out,
+    part_in,
+    left32,
+    tri32,
+    right32,
+    left_acc,
+    left_a,
+    left_b,
+    right_a,
+    right_b,
+    gate_grad,
+    proj_grad,
+    gate_acc,
+    proj_acc,
+    w_out,
+    w_in,
+    w_all,
+    tri_send,
+    tri_recv,
+    right_send,
+    right_recv,
+    part_send,
+    part_recv,
+    w_send,
+    w_recv,
+    all_send,
+    all_recv,
+):
+    row = lax.axis_index("row")
+    col = lax.axis_index("col")
+    me = row * side + col
+    team = side * side
+    width = x_ref.shape[-1]
+    piece = 4 * width // team
+    gate_piece = width // team
+    step_rows = 8
+    chunks = tile // step_rows
+    cells = step_rows * tile
+
+    barrier = pltpu.get_barrier_semaphore()
+
+    def greet(off, carry):
+        peer = lax.rem(me + off, team)
+        pl.semaphore_signal(
+            barrier,
+            inc=1,
+            device_id={"row": peer // side, "col": lax.rem(peer, side)},
+            device_id_type=MESH,
+        )
+        return carry
+
+    lax.fori_loop(1, team, greet, 0)
+
+    def spot(n):
+        return pl.ds(pl.multiple_of(n * cells, cells), cells)
+
+    def lead(n):
+        return pl.ds(n * step_rows, step_rows)
+
+    def spread_cells(ref, n):
+        part = ref[pl.ds(pl.multiple_of(n * step_rows, step_rows), step_rows), :]
+        return jnp.broadcast_to(part[:, :, None], (step_rows, tile, width)).reshape(cells, width)
+
+    gate_acc[...] = jnp.zeros_like(gate_acc)
+    proj_acc[...] = jnp.zeros_like(proj_acc)
+
+    def first(n, carry):
+        here = spot(n)
+        x = x_ref[here, :]
+        gate = jax.nn.sigmoid(jnp.dot(x, gate_ref[...], preferred_element_type=F32))
+        hat = hat_ref[here, :].astype(F32)
+        y = (hat * gain_ref[...] + bias_ref[...]).astype(BF16)
+        update = jnp.dot(y, out_ref[...], preferred_element_type=F32)
+        up = up_ref[here, :].astype(F32)
+        grad = (up * update * gate * (1.0 - gate)).astype(BF16)
+        gate_grad[here, :] = grad
+        dy = (
+            lax.dot_general(
+                (up * gate).astype(BF16), out_ref[...], LANES_DOT, preferred_element_type=F32
+            )
+            * gain_ref[...]
+        )
+        tri = spread_cells(out_rstd_ref, n) * (
+            dy
+            - jnp.mean(dy, axis=-1, keepdims=True)
+            - hat * jnp.mean(dy * hat, axis=-1, keepdims=True)
+        )
+        tri_all[col, lead(n)] = tri.astype(BF16).reshape(step_rows, tile, width)
+        return carry
+
+    lax.fori_loop(0, chunks, first, 0)
+    pl.semaphore_wait(barrier, team - 1)
+
+    def tri_copy(slot, sem, peer):
+        return pltpu.make_async_remote_copy(
+            src_ref=tri_all.at[slot],
+            dst_ref=tri_all.at[slot],
+            send_sem=tri_send.at[sem],
+            recv_sem=tri_recv.at[slot],
+            device_id={"col": peer},
+            device_id_type=MESH,
+        )
+
+    def right_copy(slot, sem, peer):
+        return pltpu.make_async_remote_copy(
+            src_ref=right_all.at[slot],
+            dst_ref=right_all.at[slot],
+            send_sem=right_send.at[sem],
+            recv_sem=right_recv.at[slot],
+            device_id={"row": peer},
+            device_id_type=MESH,
+        )
+
+    def part_copy(block, source):
+        return pltpu.make_async_remote_copy(
+            src_ref=part_out.at[block],
+            dst_ref=part_in.at[source],
+            send_sem=part_send.at[block],
+            recv_sem=part_recv.at[source],
+            device_id={"row": block},
+            device_id_type=MESH,
+        )
+
+    def w_copy(peer, source):
+        return pltpu.make_async_remote_copy(
+            src_ref=w_out.at[peer],
+            dst_ref=w_in.at[source],
+            send_sem=w_send.at[peer],
+            recv_sem=w_recv.at[source],
+            device_id={"row": peer // side, "col": lax.rem(peer, side)},
+            device_id_type=MESH,
+        )
+
+    def all_copy(peer, source):
+        return pltpu.make_async_remote_copy(
+            src_ref=w_all.at[source],
+            dst_ref=w_all.at[source],
+            send_sem=all_send.at[peer],
+            recv_sem=all_recv.at[source],
+            device_id={"row": peer // side, "col": lax.rem(peer, side)},
+            device_id_type=MESH,
+        )
+
+    half = col // 2
+    turned = col + half * (3 - 2 * col)
+
+    def block_at(s):
+        if side != 4:
+            return lax.rem(col + s, side)
+        t = s if s >= 2 else turned + s * (1 - 2 * turned)
+        return t + half * (3 - 2 * t)
+
+    for s in range(1, side):
+        tri_copy(col, s, block_at(s)).start()
+
+    col_mask = mask_ref[pl.ds(pl.multiple_of(col * tile, tile), tile), :].astype(F32)
+
+    def second(n, carry):
+        here = spot(n)
+        proj = jnp.dot(x_ref[here, :], proj_ref[...], preferred_element_type=F32)
+        at = pl.multiple_of(row * tile + n * step_rows, step_rows)
+        row_mask = mask_ref[pl.ds(at, step_rows), :].astype(F32)
+        mask = (row_mask[:, None, :] * col_mask[None, :, :]).reshape(cells, width)
+        for base, is_left in ((0, True), (2 * width, False)):
+            sig = jax.nn.sigmoid(proj[:, base : base + width])
+            value = proj[:, base + width : base + 2 * width]
+            open_ = mask * sig
+            made = (open_ * value).astype(BF16)
+            slope = open_ * value * (1.0 - sig)
+            if is_left:
+                left32[lead(n)] = made.astype(F32).reshape(step_rows, tile, width)
+                left_a[here, :] = slope
+                left_b[here, :] = open_
+            else:
+                right_all[row, lead(n)] = made.reshape(step_rows, tile, width)
+                right_a[here, :] = slope
+                right_b[here, :] = open_
+        return carry
+
+    lax.fori_loop(0, chunks, second, 0)
+    for s in range(1, side):
+        right_copy(row, s, lax.rem(row + s, side)).start()
+
+    def third(n, carry):
+        here = spot(n)
+        gate_acc[...] += lax.dot_general(
+            x_ref[here, :], gate_grad[here, :], ROWS_DOT, preferred_element_type=F32
+        )
+        return carry
+
+    lax.fori_loop(0, chunks, third, 0)
+
+    for s in range(side):
+        block = block_at(s)
+        if s > 0:
+            tri_copy(block, 0, block).wait_recv()
+        tri32[...] = tri_all[block].astype(F32)
+
+        def part_step(g, carry, block=block):
+            at = g * GROUP
+            sums = [None] * GROUP
+            for i in range(tile):
+                mine = left32[i]
+                for q in range(GROUP):
+                    term = tri32[i, pl.ds(at + q, 1), :] * mine
+                    sums[q] = term if sums[q] is None else sums[q] + term
+            for q in range(GROUP):
+                part_out[block, at + q] = sums[q].astype(BF16)
+            return carry
+
+        lax.fori_loop(0, tile // GROUP, part_step, 0)
+
+        @pl.when(block != row)
+        def _(block=block):
+            part_copy(block, row).start()
+            right_copy(block, 0, block).wait_recv()
+
+        @pl.when(block == row)
+        def _(block=block):
+            part_in[row] = part_out[block]
+
+        right32[...] = right_all[block].astype(F32)
+
+        def left_step(g, carry, s=s):
+            at = g * GROUP
+            sums = [None if s == 0 else left_acc[at + q] for q in range(GROUP)]
+            for j in range(tile):
+                mine = right32[j]
+                for q in range(GROUP):
+                    term = tri32[at + q, pl.ds(j, 1), :] * mine
+                    sums[q] = term if sums[q] is None else sums[q] + term
+            for q in range(GROUP):
+                left_acc[at + q] = sums[q]
+            return carry
+
+        lax.fori_loop(0, tile // GROUP, left_step, 0)
+
+    for s in range(1, side):
+        part_copy(row, lax.rem(row + s, side)).wait_recv()
+
+    def fourth(n, carry):
+        here = spot(n)
+        left_grad = left_acc[lead(n)].reshape(cells, width)
+        right_grad = part_in[0, lead(n)].astype(F32)
+        for r in range(1, side):
+            right_grad = right_grad + part_in[r, lead(n)].astype(F32)
+        right_grad = right_grad.reshape(cells, width)
+        x = x_ref[here, :]
+        for q, grad in enumerate(
+            (
+                left_grad * left_a[here, :],
+                left_grad * left_b[here, :],
+                right_grad * right_a[here, :],
+                right_grad * right_b[here, :],
+            )
+        ):
+            grad = grad.astype(BF16)
+            proj_grad[here, q * width : (q + 1) * width] = grad
+            proj_acc[q * width : (q + 1) * width, :] += lax.dot_general(
+                x, grad, ROWS_DOT, preferred_element_type=F32
+            )
+        return carry
+
+    lax.fori_loop(0, chunks, fourth, 0)
+
+    pad = piece + 16
+    w_out[:, 0:piece, :] = proj_acc[...].reshape(team, piece, width).astype(BF16)
+    own_gate = gate_acc[...].reshape(team, gate_piece, width)
+    w_out[:, piece:pad, :] = jnp.concatenate(
+        [own_gate, jnp.zeros((team, 16 - gate_piece, width), F32)], axis=1
+    ).astype(BF16)
+
+    def send_piece(off, carry):
+        w_copy(lax.rem(me + off, team), me).start()
+        return carry
+
+    lax.fori_loop(1, team, send_piece, 0)
+    w_in[me] = w_out[me]
+
+    def fifth(n, carry):
+        here = spot(n)
+        grad = lax.dot_general(
+            gate_grad[here, :], gate_ref[...], LANES_DOT, preferred_element_type=F32
+        ) + lax.dot_general(
+            proj_grad[here, :], proj_ref[...], LANES_DOT, preferred_element_type=F32
+        )
+        x = x_ref[here, :].astype(F32)
+        pair_out[here, :] = spread_cells(pair_rstd_ref, n) * (
+            grad
+            - jnp.mean(grad, axis=-1, keepdims=True)
+            - x * jnp.mean(grad * x, axis=-1, keepdims=True)
+        )
+        return carry
+
+    lax.fori_loop(0, chunks, fifth, 0)
+
+    def get_piece(off, carry):
+        w_copy(me, lax.rem(me + off, team)).wait_recv()
+        return carry
+
+    lax.fori_loop(1, team, get_piece, 0)
+    total = w_in[0].astype(F32)
+    for p in range(1, team):
+        total = total + w_in[p].astype(F32)
+    w_all[me] = total.astype(BF16)
+
+    def send_total(off, carry):
+        all_copy(lax.rem(me + off, team), me).start()
+        return carry
+
+    lax.fori_loop(1, team, send_total, 0)
+
+    for s in range(1, side):
+        tri_copy(col, s, block_at(s)).wait_send()
+        right_copy(row, s, lax.rem(row + s, side)).wait_send()
+        part_copy(lax.rem(row + s, side), row).wait_send()
+
+    def finish(off, carry):
+        w_copy(lax.rem(me + off, team), me).wait_send()
+        return carry
+
+    lax.fori_loop(1, team, finish, 0)
+
+    def get_total(off, carry):
+        peer = lax.rem(me + off, team)
+        all_copy(me, peer).wait_recv()
+        return carry
+
+    lax.fori_loop(1, team, get_total, 0)
+
+    def finish_total(off, carry):
+        all_copy(lax.rem(me + off, team), me).wait_send()
+        return carry
+
+    lax.fori_loop(1, team, finish_total, 0)
+
+    each = width // piece
+    for q in range(4):
+        proj_out[:, q * width : (q + 1) * width] = (
+            w_all[q * each : (q + 1) * each, 0:piece, :].astype(F32).reshape(width, width)
+        )
+    gate_out[...] = w_all[:, piece:pad, :].astype(F32)[:, 0:gate_piece, :].reshape(width, width)
+
+
+def fused(
+    pair_norm,
+    pair_rstd,
+    out_norm,
+    out_rstd,
+    grad_out,
+    token_mask,
+    proj_weight,
+    gate_weight,
+    out_weight,
+    out_gain,
+    out_bias,
+):
+    tile, _, width = pair_norm.shape
+    side = lax.axis_size("row")
+    team = side * side
+    cells = tile * tile
+    piece = 4 * width // team + 16
+    vmem = pl.BlockSpec(memory_space=pltpu.VMEM)
+    dma = pltpu.SemaphoreType.DMA
+    tokens = token_mask.shape[0]
+    mask = jnp.broadcast_to(token_mask[:, None], (tokens, width))
+    pair_grad, proj_wgrad, gate_wgrad = pl.pallas_call(
+        functools.partial(kernel, side, tile),
+        out_shape=(
+            jax.ShapeDtypeStruct((cells, width), F32),
+            jax.ShapeDtypeStruct((width, 4 * width), F32),
+            jax.ShapeDtypeStruct((width, width), F32),
+        ),
+        in_specs=[vmem] * 11,
+        out_specs=(vmem, vmem, vmem),
+        scratch_shapes=[
+            pltpu.VMEM((side, tile, tile, width), BF16),
+            pltpu.VMEM((side, tile, tile, width), BF16),
+            pltpu.VMEM((side, tile, tile, width), BF16),
+            pltpu.VMEM((side, tile, tile, width), BF16),
+            pltpu.VMEM((tile, tile, width), F32),
+            pltpu.VMEM((tile, tile, width), F32),
+            pltpu.VMEM((tile, tile, width), F32),
+            pltpu.VMEM((tile, tile, width), F32),
+            pltpu.VMEM((cells, width), F32),
+            pltpu.VMEM((cells, width), F32),
+            pltpu.VMEM((cells, width), F32),
+            pltpu.VMEM((cells, width), F32),
+            pltpu.VMEM((cells, width), BF16),
+            pltpu.VMEM((cells, 4 * width), BF16),
+            pltpu.VMEM((width, width), F32),
+            pltpu.VMEM((4 * width, width), F32),
+            pltpu.VMEM((team, piece, width), BF16),
+            pltpu.VMEM((team, piece, width), BF16),
+            pltpu.VMEM((team, piece, width), BF16),
+            dma((side,)),
+            dma((side,)),
+            dma((side,)),
+            dma((side,)),
+            dma((side,)),
+            dma((side,)),
+            dma((team,)),
+            dma((team,)),
+            dma((team,)),
+            dma((team,)),
+        ],
+        compiler_params=pltpu.CompilerParams(
+            collective_id=0, has_side_effects=True, vmem_limit_bytes=40 * 1024 * 1024
+        ),
+    )(
+        pair_norm.reshape(cells, width),
+        pair_rstd,
+        out_norm.reshape(cells, width),
+        out_rstd,
+        grad_out.reshape(cells, width),
+        mask,
+        proj_weight,
+        gate_weight,
+        out_weight,
+        out_gain.reshape(1, width),
+        out_bias.reshape(1, width),
+    )
+    return pair_grad.reshape(tile, tile, width), proj_wgrad, gate_wgrad
+
+
+def local(pair_norm, *rest):
+    rows, cols = lax.axis_size("row"), lax.axis_size("col")
+    tile_rows, tile_cols, width = pair_norm.shape
+    hidden = rest[7].shape[0]
+    team = rows * cols
+    fits = (
+        rows == cols
+        and tile_rows == tile_cols
+        and tile_rows % 16 == 0
+        and tile_rows <= 32
+        and hidden == width
+        and width == 128
+        and 8 <= team <= 32
+        and width % team == 0
+        and 4 * width // team % 16 == 0
+    )
+    return (fused if fits else plain)(pair_norm, *rest)
+
+
 def solution(mesh):
     placed = (
         P(("groups", "row"), "col", None),

time: 262 us -> 67.4 us (0.26)
  waiting for transfers between devices: 191 us -> 0 us
  Pallas kernels: 0 us -> 57.6 us
  local copies, waits for them, and re-layouts: 31.6 us -> 8.72 us
  matrix products: 18.4 us -> 0 us
  between operations: 14.4 us -> 0.68 us
  other arithmetic: 5.29 us -> 0 us
    psum x2 -> x0, waiting for transfers between devices: 134 us -> none  [the longest x1 86.9 us: local(): proj_wgrad, gate_wgrad = lax.psum((proj_part, gate_part), ('row', 'col'))]
    pallas_call x0 -> x1, Pallas kernels: none -> 57.6 us  [fused(): pl.pallas_call(functools.partial(kernel, side, tile), out_shape=(jax.Shap...]
    all_gather x4 -> x0, waiting for transfers between devices: 56.6 us -> none  [the longest x1 22.3 us: local(): lax.all_gather(tri_grad, 'col', axis=1, tiled=True)]
    all_gather x4 -> x0, local copies, waits for them, and re-layouts: 19.4 us -> none  [the longest x1 7.23 us: local(): lax.all_gather(right_proj, 'row', axis=0, tiled=True)]
    dot_general x10 -> x0, matrix products: 18.4 us -> none  [the longest x1 5.07 us: local(): lax.dot_general(panel, left_cols, (((0,), (0,)), ((2,), (2,))), preferred...]
    dot_general x2 -> x0, local copies, waits for them, and re-layouts: 5.41 us -> none  [the longest x1 2.76 us: local(): lax.dot_general(lax.all_gather(tri_grad, 'col', axis=1, tiled=True), righ...]
    unnamed x36 -> x25, local copies, waits for them, and re-layouts: 4.35 us -> 8.65 us
  transfers between devices with their start and end apart: 6 -> 0, of which waited for: 6 -> 0; matrix products, arithmetic and copies ran while one was open for 14% -> 0% of each run, Pallas kernels for 0% -> 0%
where the time goes in v1:
time: 67.4 us; the launch traced here: 67 us
  Pallas kernels  57.6 us (85%)
  local copies, waits for them, and re-layouts  8.72 us (13%)
  between operations  0.68 us (1%)
    pallas_call x1, Pallas kernels, fused(): pl.pallas_call(functools.partial(kernel, side, tile), out_shape=(jax.Shap...  57.6 us
    unnamed x25, local copies, waits for them, and re-layouts  8.65 us

profile of v1, /device:TPU:0, one launch (start us, length us, event | category | flops | bytes accessed | tf_op | source)
XLA Modules:
  0.0 67.0 jit_solution(8118105520877215735)
XLA Ops:
  0.6 0.0 copy-start.10
  0.6 0.0 copy-start.9
  0.7 0.6 copy-done.10
  1.3 0.0 copy-start.4
  1.3 0.0 copy-start.5
  1.3 0.0 copy-start.8
  1.3 0.1 broadcast_in_dim.2.mask_ref
  1.4 0.0 copy-done.9
  1.4 0.7 copy-done.4
  2.0 0.0 copy-done.5
  2.1 0.0 copy-done.8
  2.1 0.0 copy-start
  2.1 0.9 %copy-done = bf16[32,32,128]{2,1,0:T(8,128)(2,1)S(1)} copy-done((bf16[32,32,128]{2,1,0:T(8,128)(2,1)S(1)}, bf16[32,32,128]{2,1,0:T(8,128)(2,1)}, u32[]{:S(2)}) %copy-start) | copy-done | bytes 262168
  3.0 0.0 copy-start.1
  3.0 0.9 %copy-done.1 = bf16[32,32,128]{2,1,0:T(8,128)(2,1)S(1)} copy-done((bf16[32,32,128]{2,1,0:T(8,128)(2,1)S(1)}, bf16[32,32,128]{2,1,0:T(8,128)(2,1)}, u32[]{:S(2)}) %copy-start.1) | copy-done | bytes 262168
  4.0 0.0 copy-start.2
  4.0 0.9 %copy-done.2 = bf16[32,32,128]{2,1,0:T(8,128)(2,1)S(1)} copy-done((bf16[32,32,128]{2,1,0:T(8,128)(2,1)S(1)}, bf16[32,32,128]{2,1,0:T(8,128)(2,1)}, u32[]{:S(2)}) %copy-start.2) | copy-done | bytes 262168
  4.9 0.0 copy-start.3
  4.9 0.9 %copy-done.3 = bf16[128,512]{1,0:T(8,128)(2,1)S(1)} copy-done((bf16[128,512]{1,0:T(8,128)(2,1)S(1)}, bf16[128,512]{1,0:T(8,128)(2,1)}, u32[]{:S(2)}) %copy-start.3) | copy-done | bytes 131096
  5.8 0.0 copy-start.6
  5.8 0.7 %copy-done.6 = f32[32,32]{1,0:T(8,128)S(1)} copy-done((f32[32,32]{1,0:T(8,128)S(1)}, f32[32,32]{1,0:T(8,128)}, u32[]{:S(2)}) %copy-start.6) | copy-done | bytes 4120
  6.5 0.0 copy-start.7
  6.5 0.7 %copy-done.7 = f32[32,32]{1,0:T(8,128)S(1)} copy-done((f32[32,32]{1,0:T(8,128)S(1)}, f32[32,32]{1,0:T(8,128)}, u32[]{:S(2)}) %copy-start.7) | copy-done | bytes 4120
  7.3 57.6 %shard_map.130 = (f32[1024,128]{1,0:T(8,128)S(1)}, f32[128,512]{1,0:T(8,128)S(1)}, f32[128,128]{1,0:T(8,128)S(1)}) custom-call(bf16[1024,128]{1,0:T(8,128)(2,1)S(1)} %bitcast.7, f32[32,32]{1,0:T(8,128)S(1)} %copy-done.6, bf16[1024,128]{1,0:T(8,128)(2,1)S(1)} %bitcast.8, f32[32,32]{1,0:T(8,128)S(1)} %copy-done.7, bf16[1024,128]{1,0:T(8,128)(2,1)S(1)} %bitcast.9, ...), custom_call_target="tpu_custom_call" | custom-call | tf_op jit(solution)/shard_map/pallas_call | solution.py:518
  64.8 0.8 %copy.17 = f32[32,32,128]{2,1,0:T(8,128)} copy(f32[32,32,128]{2,1,0:T(8,128)S(1)} %bitcast.6) | data formatting | bytes 1048576
  65.6 0.7 %copy.18 = f32[128,512]{1,0:T(8,128)} copy(f32[128,512]{1,0:T(8,128)S(1)} %get-tuple-element.13) | data formatting | bytes 524288
  66.3 0.6 copy.19
Async XLA Ops:
  0.6 0.7 copy-start.10
  0.6 0.7 %copy-start.9 = (f32[128]{0:T(128)S(1)}, f32[128]{0:T(128)}, u32[]{:S(2)}) copy-start(f32[128]{0:T(128)} %param.21) | copy-start | bytes 1540
  1.3 0.8 %copy-start.4 = (bf16[128,128]{1,0:T(8,128)(2,1)S(1)}, bf16[128,128]{1,0:T(8,128)(2,1)}, u32[]{:S(2)}) copy-start(bf16[128,128]{1,0:T(8,128)(2,1)} %gate_ref.1) | copy-start | bytes 98308
  1.3 0.8 %copy-start.5 = (bf16[128,128]{1,0:T(8,128)(2,1)S(1)}, bf16[128,128]{1,0:T(8,128)(2,1)}, u32[]{:S(2)}) copy-start(bf16[128,128]{1,0:T(8,128)(2,1)} %out_ref.1) | copy-start | bytes 98308
  1.3 0.8 %copy-start.8 = (f32[128]{0:T(128)S(1)}, f32[128]{0:T(128)}, u32[]{:S(2)}) copy-start(f32[128]{0:T(128)} %param.20) | copy-start | bytes 1540
  2.1 1.0 %copy-start = (bf16[32,32,128]{2,1,0:T(8,128)(2,1)S(1)}, bf16[32,32,128]{2,1,0:T(8,128)(2,1)}, u32[]{:S(2)}) copy-start(bf16[32,32,128]{2,1,0:T(8,128)(2,1)} %param.11) | copy-start | bytes 786436
  3.0 0.9 %copy-start.1 = (bf16[32,32,128]{2,1,0:T(8,128)(2,1)S(1)}, bf16[32,32,128]{2,1,0:T(8,128)(2,1)}, u32[]{:S(2)}) copy-start(bf16[32,32,128]{2,1,0:T(8,128)(2,1)} %param.13) | copy-start | bytes 786436
  4.0 0.9 %copy-start.2 = (bf16[32,32,128]{2,1,0:T(8,128)(2,1)S(1)}, bf16[32,32,128]{2,1,0:T(8,128)(2,1)}, u32[]{:S(2)}) copy-start(bf16[32,32,128]{2,1,0:T(8,128)(2,1)} %param.15) | copy-start | bytes 786436
  4.9 0.9 %copy-start.3 = (bf16[128,512]{1,0:T(8,128)(2,1)S(1)}, bf16[128,512]{1,0:T(8,128)(2,1)}, u32[]{:S(2)}) copy-start(bf16[128,512]{1,0:T(8,128)(2,1)} %proj_ref.1) | copy-start | bytes 393220
  5.8 0.7 %copy-start.6 = (f32[32,32]{1,0:T(8,128)S(1)}, f32[32,32]{1,0:T(8,128)}, u32[]{:S(2)}) copy-start(f32[32,32]{1,0:T(8,128)} %pair_rstd_ref.1) | copy-start | bytes 12292
  6.5 0.7 %copy-start.7 = (f32[32,32]{1,0:T(8,128)S(1)}, f32[32,32]{1,0:T(8,128)}, u32[]{:S(2)}) copy-start(f32[32,32]{1,0:T(8,128)} %out_rstd_ref.1) | copy-start | bytes 12292

commit v2 on v1

--- a/solution.py
+++ b/solution.py
@@ -133,24 +133,37 @@
 def kernel(
     side,
     tile,
+    x_hbm,
+    pair_rstd_hbm,
+    hat_hbm,
+    out_rstd_hbm,
+    up_hbm,
+    mask_hbm,
+    proj_hbm,
+    gate_hbm,
+    out_hbm,
+    gain_hbm,
+    bias_hbm,
+    pair_out,
+    proj_out,
+    gate_out,
     x_ref,
     pair_rstd_ref,
     hat_ref,
     out_rstd_ref,
     up_ref,
-    mask_ref,
+    mask_in,
     proj_ref,
     gate_ref,
     out_ref,
     gain_ref,
     bias_ref,
-    pair_out,
-    proj_out,
-    gate_out,
+    mask_ref,
     tri_all,
     right_all,
     part_out,
     part_in,
+    relay_in,
     left32,
     tri32,
     right32,
@@ -166,37 +179,61 @@
     w_out,
     w_in,
     w_all,
+    load_sem,
     tri_send,
     tri_recv,
     right_send,
     right_recv,
     part_send,
     part_recv,
+    relay_recv,
     w_send,
     w_recv,
     all_send,
     all_recv,
 ):
+    loads = [
+        pltpu.make_async_copy(source, target, load_sem.at[k])
+        for k, (source, target) in enumerate(
+            (
+                (x_hbm, x_ref),
+                (hat_hbm, hat_ref),
+                (up_hbm, up_ref),
+                (gate_hbm, gate_ref),
+                (out_hbm, out_ref),
+                (out_rstd_hbm, out_rstd_ref),
+                (gain_hbm, gain_ref),
+                (bias_hbm, bias_ref),
+                (mask_hbm, mask_in),
+                (proj_hbm, proj_ref),
+                (pair_rstd_hbm, pair_rstd_ref),
+            )
+        )
+    ]
+    for load in loads:
+        load.start()
+
     row = lax.axis_index("row")
     col = lax.axis_index("col")
     me = row * side + col
     team = side * side
     width = x_ref.shape[-1]
-    piece = 4 * width // team
-    gate_piece = width // team
     step_rows = 8
     chunks = tile // step_rows
     cells = step_rows * tile
+    part = tile // 2
+    sibling = row + 1 - 2 * lax.rem(row, 2)
+    across = lax.rem(row + 2, side)
+    beyond = lax.rem(sibling + 2, side)
 
     barrier = pltpu.get_barrier_semaphore()
 
+    def place(peer):
+        return {"row": peer // side, "col": lax.rem(peer, side)}
+
     def greet(off, carry):
-        peer = lax.rem(me + off, team)
         pl.semaphore_signal(
-            barrier,
-            inc=1,
-            device_id={"row": peer // side, "col": lax.rem(peer, side)},
-            device_id_type=MESH,
+            barrier, inc=1, device_id=place(lax.rem(me + off, team)), device_id_type=MESH
         )
         return carry
 
@@ -209,11 +246,74 @@
         return pl.ds(n * step_rows, step_rows)
 
     def spread_cells(ref, n):
-        part = ref[pl.ds(pl.multiple_of(n * step_rows, step_rows), step_rows), :]
-        return jnp.broadcast_to(part[:, :, None], (step_rows, tile, width)).reshape(cells, width)
+        rows = ref[pl.ds(pl.multiple_of(n * step_rows, step_rows), step_rows), :]
+        return jnp.broadcast_to(rows[:, :, None], (step_rows, tile, width)).reshape(cells, width)
+
+    def remote(source, target, send, recv, where):
+        return pltpu.make_async_remote_copy(
+            src_ref=source,
+            dst_ref=target,
+            send_sem=send,
+            recv_sem=recv,
+            device_id=where,
+            device_id_type=MESH,
+        )
+
+    def tri_copy(slot, h, sem, peer):
+        piece = tri_all.at[slot, :, pl.ds(h * part, part), :]
+        return remote(piece, piece, tri_send.at[sem, h], tri_recv.at[slot, h], {"col": peer})
+
+    def right_copy(slot, sem, peer):
+        return remote(
+            right_all.at[slot],
+            right_all.at[slot],
+            right_send.at[sem],
+            right_recv.at[slot],
+            {"row": peer},
+        )
+
+    def part_copy(block, h, kind, peer):
+        here = pl.ds(h * part, part)
+        return remote(
+            part_out.at[block, here],
+            part_in.at[kind, here],
+            part_send.at[block, h],
+            part_recv.at[kind, h],
+            {"row": peer},
+        )
+
+    def relay_copy(block, h):
+        here = pl.ds(h * part, part)
+        return remote(
+            part_out.at[block, here],
+            relay_in.at[here],
+            part_send.at[block, h],
+            relay_recv.at[h],
+            {"row": sibling},
+        )
+
+    def w_copy(k, peer, source):
+        return remote(
+            w_out.at[k, peer],
+            w_in.at[k, source],
+            w_send.at[k, peer],
+            w_recv.at[k, source],
+            place(peer),
+        )
+
+    def all_copy(k, peer, source):
+        return remote(
+            w_all.at[k, source],
+            w_all.at[k, source],
+            all_send.at[k, peer],
+            all_recv.at[k, source],
+            place(peer),
+        )
 
     gate_acc[...] = jnp.zeros_like(gate_acc)
     proj_acc[...] = jnp.zeros_like(proj_acc)
+    for load in loads[:8]:
+        load.wait()
 
     def first(n, carry):
         here = spot(n)
@@ -240,77 +340,49 @@
         return carry
 
     lax.fori_loop(0, chunks, first, 0)
+    for load in loads[8:]:
+        load.wait()
     pl.semaphore_wait(barrier, team - 1)
 
-    def tri_copy(slot, sem, peer):
-        return pltpu.make_async_remote_copy(
-            src_ref=tri_all.at[slot],
-            dst_ref=tri_all.at[slot],
-            send_sem=tri_send.at[sem],
-            recv_sem=tri_recv.at[slot],
-            device_id={"col": peer},
-            device_id_type=MESH,
-        )
-
-    def right_copy(slot, sem, peer):
-        return pltpu.make_async_remote_copy(
-            src_ref=right_all.at[slot],
-            dst_ref=right_all.at[slot],
-            send_sem=right_send.at[sem],
-            recv_sem=right_recv.at[slot],
-            device_id={"row": peer},
-            device_id_type=MESH,
-        )
-
-    def part_copy(block, source):
-        return pltpu.make_async_remote_copy(
-            src_ref=part_out.at[block],
-            dst_ref=part_in.at[source],
-            send_sem=part_send.at[block],
-            recv_sem=part_recv.at[source],
-            device_id={"row": block},
-            device_id_type=MESH,
-        )
-
-    def w_copy(peer, source):
-        return pltpu.make_async_remote_copy(
-            src_ref=w_out.at[peer],
-            dst_ref=w_in.at[source],
-            send_sem=w_send.at[peer],
-            recv_sem=w_recv.at[source],
-            device_id={"row": peer // side, "col": lax.rem(peer, side)},
-            device_id_type=MESH,
-        )
-
-    def all_copy(peer, source):
-        return pltpu.make_async_remote_copy(
-            src_ref=w_all.at[source],
-            dst_ref=w_all.at[source],
-            send_sem=all_send.at[peer],
-            recv_sem=all_recv.at[source],
-            device_id={"row": peer // side, "col": lax.rem(peer, side)},
-            device_id_type=MESH,
-        )
-
-    half = col // 2
-    turned = col + half * (3 - 2 * col)
+    upper = col // 2
+    inner = lax.rem(col + upper, 2)
+
+    def mirror(t):
+        return t + upper * (3 - 2 * t)
 
     def block_at(s):
-        if side != 4:
-            return lax.rem(col + s, side)
-        t = s if s >= 2 else turned + s * (1 - 2 * turned)
-        return t + half * (3 - 2 * t)
-
-    for s in range(1, side):
-        tri_copy(col, s, block_at(s)).start()
-
-    col_mask = mask_ref[pl.ds(pl.multiple_of(col * tile, tile), tile), :].astype(F32)
+        return mirror(s if s >= 2 else inner + s * (1 - 2 * inner))
+
+    toward_end, toward_middle = mirror(0), mirror(inner + 1)
+
+    for h in range(2):
+        tri_copy(col, h, 0, toward_middle).start()
+
+        @pl.when(inner == 1)
+        def _(h=h):
+            tri_copy(col, h, 1, toward_end).start()
+
+    def forward_to(s):
+        return toward_middle if s == 1 else toward_end
+
+    def take_tri(s, h):
+        block = block_at(s)
+        tri_copy(block, h, 0, block).wait_recv()
+
+        @pl.when(inner == 1)
+        def _():
+            tri_copy(block, h, s + 1, forward_to(s)).start()
+
+    mask_ref[...] = jnp.transpose(
+        jnp.broadcast_to(mask_in[...].astype(F32), (width, mask_in.shape[-1]))
+    )
+    col_mask = mask_ref[pl.ds(pl.multiple_of(col * tile, tile), tile), :]
 
     def second(n, carry):
         here = spot(n)
         proj = jnp.dot(x_ref[here, :], proj_ref[...], preferred_element_type=F32)
         at = pl.multiple_of(row * tile + n * step_rows, step_rows)
-        row_mask = mask_ref[pl.ds(at, step_rows), :].astype(F32)
+        row_mask = mask_ref[pl.ds(at, step_rows), :]
         mask = (row_mask[:, None, :] * col_mask[None, :, :]).reshape(cells, width)
         for base, is_left in ((0, True), (2 * width, False)):
             sig = jax.nn.sigmoid(proj[:, base : base + width])
@@ -329,26 +401,16 @@
         return carry
 
     lax.fori_loop(0, chunks, second, 0)
-    for s in range(1, side):
-        right_copy(row, s, lax.rem(row + s, side)).start()
-
-    def third(n, carry):
-        here = spot(n)
-        gate_acc[...] += lax.dot_general(
-            x_ref[here, :], gate_grad[here, :], ROWS_DOT, preferred_element_type=F32
-        )
-        return carry
-
-    lax.fori_loop(0, chunks, third, 0)
-
-    for s in range(side):
+    right_copy(row, 0, across).start()
+    right_copy(row, 1, sibling).start()
+
+    def do_part(s, h):
         block = block_at(s)
-        if s > 0:
-            tri_copy(block, 0, block).wait_recv()
-        tri32[...] = tri_all[block].astype(F32)
-
-        def part_step(g, carry, block=block):
-            at = g * GROUP
+        span = pl.ds(h * part, part)
+        tri32[:, span, :] = tri_all[block, :, span, :].astype(F32)
+
+        def body(g, carry):
+            at = h * part + g * GROUP
             sums = [None] * GROUP
             for i in range(tile):
                 mine = left32[i]
@@ -359,20 +421,33 @@
                 part_out[block, at + q] = sums[q].astype(BF16)
             return carry
 
-        lax.fori_loop(0, tile // GROUP, part_step, 0)
-
-        @pl.when(block != row)
-        def _(block=block):
-            part_copy(block, row).start()
-            right_copy(block, 0, block).wait_recv()
-
-        @pl.when(block == row)
-        def _(block=block):
-            part_in[row] = part_out[block]
-
+        lax.fori_loop(0, part // GROUP, body, 0)
+
+        @pl.when(block == sibling)
+        def _():
+            part_copy(block, h, 0, sibling).start()
+
+        @pl.when(block == beyond)
+        def _():
+            relay_copy(block, h).start()
+
+    def do_relay(s, h):
+        block = block_at(s)
+        span = pl.ds(h * part, part)
+
+        @pl.when(block == across)
+        def _():
+            relay_copy(block, h).wait_recv()
+            part_out[block, span] = (
+                part_out[block, span].astype(F32) + relay_in[span].astype(F32)
+            ).astype(BF16)
+            part_copy(block, h, 1, across).start()
+
+    def do_left(s):
+        block = block_at(s)
         right32[...] = right_all[block].astype(F32)
 
-        def left_step(g, carry, s=s):
+        def body(g, carry):
             at = g * GROUP
             sums = [None if s == 0 else left_acc[at + q] for q in range(GROUP)]
             for j in range(tile):
@@ -384,51 +459,115 @@
                 left_acc[at + q] = sums[q]
             return carry
 
-        lax.fori_loop(0, tile // GROUP, left_step, 0)
-
+        lax.fori_loop(0, tile // GROUP, body, 0)
+
+    for h in range(2):
+        do_part(0, h)
+
+    def third(n, carry):
+        here = spot(n)
+        gate_acc[...] += lax.dot_general(
+            x_ref[here, :], gate_grad[here, :], ROWS_DOT, preferred_element_type=F32
+        )
+        return carry
+
+    lax.fori_loop(0, chunks, third, 0)
+    for h in range(2):
+        do_relay(0, h)
+    for h in range(2):
+        take_tri(1, h)
+    right_copy(across, 0, across).wait_recv()
+    right_copy(across, 2, sibling).start()
+    right_copy(sibling, 0, sibling).wait_recv()
+    right_copy(beyond, 0, sibling).wait_recv()
+    do_left(0)
     for s in range(1, side):
-        part_copy(row, lax.rem(row + s, side)).wait_recv()
-
-    def fourth(n, carry):
+        for h in range(2):
+            if s > 1:
+                take_tri(s, h)
+            do_part(s, h)
+        if s < side - 1:
+            do_left(s)
+        for h in range(2):
+            do_relay(s, h)
+        if s == side - 1:
+            do_left(s)
+
+    def weights(n, grads, base):
         here = spot(n)
-        left_grad = left_acc[lead(n)].reshape(cells, width)
-        right_grad = part_in[0, lead(n)].astype(F32)
-        for r in range(1, side):
-            right_grad = right_grad + part_in[r, lead(n)].astype(F32)
-        right_grad = right_grad.reshape(cells, width)
         x = x_ref[here, :]
-        for q, grad in enumerate(
-            (
-                left_grad * left_a[here, :],
-                left_grad * left_b[here, :],
-                right_grad * right_a[here, :],
-                right_grad * right_b[here, :],
-            )
-        ):
+        for q, grad in enumerate(grads):
             grad = grad.astype(BF16)
-            proj_grad[here, q * width : (q + 1) * width] = grad
-            proj_acc[q * width : (q + 1) * width, :] += lax.dot_general(
+            at = (base + q) * width
+            proj_grad[here, at : at + width] = grad
+            proj_acc[at : at + width, :] += lax.dot_general(
                 x, grad, ROWS_DOT, preferred_element_type=F32
             )
-        return carry
-
-    lax.fori_loop(0, chunks, fourth, 0)
-
-    pad = piece + 16
-    w_out[:, 0:piece, :] = proj_acc[...].reshape(team, piece, width).astype(BF16)
-    own_gate = gate_acc[...].reshape(team, gate_piece, width)
-    w_out[:, piece:pad, :] = jnp.concatenate(
-        [own_gate, jnp.zeros((team, 16 - gate_piece, width), F32)], axis=1
+
+    def left_weights(n, carry):
+        here = spot(n)
+        grad = left_acc[lead(n)].reshape(cells, width)
+        weights(n, (grad * left_a[here, :], grad * left_b[here, :]), 0)
+        return carry
+
+    def right_weights(n, carry):
+        here = spot(n)
+        grad = part_out[row, lead(n)].astype(F32)
+        for kind in range(2):
+            grad = grad + part_in[kind, lead(n)].astype(F32)
+        grad = grad.reshape(cells, width)
+        weights(n, (grad * right_a[here, :], grad * right_b[here, :]), 2)
+        return carry
+
+    piece = 2 * width // team
+    gate_piece = width // team
+
+    def send_pieces(k):
+        half = proj_acc[2 * k * width : 2 * (k + 1) * width, :]
+        w_out[k, :, 0:piece, :] = half.reshape(team, piece, width).astype(BF16)
+
+        def body(off, carry):
+            w_copy(k, lax.rem(me + off, team), me).start()
+            return carry
+
+        lax.fori_loop(1, team, body, 0)
+        w_in[k, me] = w_out[k, me]
+
+    def send_totals(k):
+        def body(off, carry):
+            w_copy(k, me, lax.rem(me + off, team)).wait_recv()
+            return carry
+
+        lax.fori_loop(1, team, body, 0)
+        total = w_in[k, 0].astype(F32)
+        for p in range(1, team):
+            total = total + w_in[k, p].astype(F32)
+        w_all[k, me] = total.astype(BF16)
+
+        def push(off, carry):
+            all_copy(k, lax.rem(me + off, team), me).start()
+            return carry
+
+        lax.fori_loop(1, team, push, 0)
+
+    lax.fori_loop(0, chunks, left_weights, 0)
+    w_out[0, :, piece : piece + 16, :] = jnp.concatenate(
+        [
+            gate_acc[...].reshape(team, gate_piece, width),
+            jnp.zeros((team, 16 - gate_piece, width), F32),
+        ],
+        axis=1,
     ).astype(BF16)
-
-    def send_piece(off, carry):
-        w_copy(lax.rem(me + off, team), me).start()
-        return carry
-
-    lax.fori_loop(1, team, send_piece, 0)
-    w_in[me] = w_out[me]
-
-    def fifth(n, carry):
+    w_out[1, :, piece : piece + 16, :] = jnp.zeros((team, 16, width), BF16)
+    send_pieces(0)
+    for kind in range(2):
+        for h in range(2):
+            part_copy(row, h, kind, sibling).wait_recv()
+    lax.fori_loop(0, chunks, right_weights, 0)
+    send_pieces(1)
+    send_totals(0)
+
+    def last(n, carry):
         here = spot(n)
         grad = lax.dot_general(
             gate_grad[here, :], gate_ref[...], LANES_DOT, preferred_element_type=F32
@@ -443,54 +582,78 @@
         )
         return carry
 
-    lax.fori_loop(0, chunks, fifth, 0)
-
-    def get_piece(off, carry):
-        w_copy(me, lax.rem(me + off, team)).wait_recv()
-        return carry
-
-    lax.fori_loop(1, team, get_piece, 0)
-    total = w_in[0].astype(F32)
-    for p in range(1, team):
-        total = total + w_in[p].astype(F32)
-    w_all[me] = total.astype(BF16)
-
-    def send_total(off, carry):
-        all_copy(lax.rem(me + off, team), me).start()
-        return carry
-
-    lax.fori_loop(1, team, send_total, 0)
-
-    for s in range(1, side):
-        tri_copy(col, s, block_at(s)).wait_send()
-        right_copy(row, s, lax.rem(row + s, side)).wait_send()
-        part_copy(lax.rem(row + s, side), row).wait_send()
+    lax.fori_loop(0, chunks // 2, last, 0)
+    send_totals(1)
+    lax.fori_loop(chunks // 2, chunks, last, 0)
+
+    for h in range(2):
+        tri_copy(col, h, 0, toward_middle).wait_send()
+
+        @pl.when(inner == 1)
+        def _(h=h):
+            tri_copy(col, h, 1, toward_end).wait_send()
+            for s in range(1, side):
+                tri_copy(block_at(s), h, s + 1, forward_to(s)).wait_send()
+
+        part_copy(sibling, h, 0, sibling).wait_send()
+        relay_copy(beyond, h).wait_send()
+        part_copy(across, h, 1, across).wait_send()
+    right_copy(row, 0, across).wait_send()
+    right_copy(row, 1, sibling).wait_send()
+    right_copy(across, 2, sibling).wait_send()
 
     def finish(off, carry):
-        w_copy(lax.rem(me + off, team), me).wait_send()
+        peer = lax.rem(me + off, team)
+        for k in range(2):
+            w_copy(k, peer, me).wait_send()
         return carry
 
     lax.fori_loop(1, team, finish, 0)
 
-    def get_total(off, carry):
+    def get_totals(off, carry):
         peer = lax.rem(me + off, team)
-        all_copy(me, peer).wait_recv()
-        return carry
-
-    lax.fori_loop(1, team, get_total, 0)
-
-    def finish_total(off, carry):
-        all_copy(lax.rem(me + off, team), me).wait_send()
-        return carry
-
-    lax.fori_loop(1, team, finish_total, 0)
+        for k in range(2):
+            all_copy(k, me, peer).wait_recv()
+        return carry
+
+    lax.fori_loop(1, team, get_totals, 0)
+
+    def finish_totals(off, carry):
+        peer = lax.rem(me + off, team)
+        for k in range(2):
+            all_copy(k, peer, me).wait_send()
+        return carry
+
+    lax.fori_loop(1, team, finish_totals, 0)
 
     each = width // piece
     for q in range(4):
+        k, at = q // 2, (q % 2) * each
         proj_out[:, q * width : (q + 1) * width] = (
-            w_all[q * each : (q + 1) * each, 0:piece, :].astype(F32).reshape(width, width)
-        )
-    gate_out[...] = w_all[:, piece:pad, :].astype(F32)[:, 0:gate_piece, :].reshape(width, width)
+            w_all[k, at : at + each, 0:piece, :].astype(F32).reshape(width, width)
+        )
+    gate_out[...] = (
+        w_all[0, :, piece : piece + 16, :].astype(F32)[:, 0:gate_piece, :].reshape(width, width)
+    )
+
+
+def flush(*refs):
+    count = len(refs) // 3
+    sources, targets, held = refs[:count], refs[count : 2 * count], refs[2 * count : -1]
+    sem = refs[-1]
+    reads = [
+        pltpu.make_async_copy(sources[k], held[k], sem.at[0, k]) for k in range(count)
+    ]
+    writes = [
+        pltpu.make_async_copy(held[k], targets[k], sem.at[1, k]) for k in range(count)
+    ]
+    for read in reads:
+        read.start()
+    for read, write in zip(reads, writes):
+        read.wait()
+        write.start()
+    for write in writes:
+        write.wait()
 
 
 def fused(
@@ -510,25 +673,42 @@
     side = lax.axis_size("row")
     team = side * side
     cells = tile * tile
-    piece = 4 * width // team + 16
+    piece = 2 * width // team + 16
+    tokens = token_mask.shape[0]
     vmem = pl.BlockSpec(memory_space=pltpu.VMEM)
+    hbm = pl.BlockSpec(memory_space=pltpu.HBM)
     dma = pltpu.SemaphoreType.DMA
-    tokens = token_mask.shape[0]
-    mask = jnp.broadcast_to(token_mask[:, None], (tokens, width))
-    pair_grad, proj_wgrad, gate_wgrad = pl.pallas_call(
+    shapes = (
+        jax.ShapeDtypeStruct((cells, width), F32),
+        jax.ShapeDtypeStruct((width, 4 * width), F32),
+        jax.ShapeDtypeStruct((width, width), F32),
+    )
+    arrays = (
+        pair_norm.reshape(cells, width),
+        pair_rstd,
+        out_norm.reshape(cells, width),
+        out_rstd,
+        grad_out.reshape(cells, width),
+        token_mask.reshape(1, tokens),
+        proj_weight,
+        gate_weight,
+        out_weight,
+        out_gain.reshape(1, width),
+        out_bias.reshape(1, width),
+    )
+    made = pl.pallas_call(
         functools.partial(kernel, side, tile),
-        out_shape=(
-            jax.ShapeDtypeStruct((cells, width), F32),
-            jax.ShapeDtypeStruct((width, 4 * width), F32),
-            jax.ShapeDtypeStruct((width, width), F32),
-        ),
-        in_specs=[vmem] * 11,
+        out_shape=shapes,
+        in_specs=[hbm] * 11,
         out_specs=(vmem, vmem, vmem),
-        scratch_shapes=[
+        scratch_shapes=[pltpu.VMEM(a.shape, a.dtype) for a in arrays]
+        + [
+            pltpu.VMEM((tokens, width), F32),
             pltpu.VMEM((side, tile, tile, width), BF16),
             pltpu.VMEM((side, tile, tile, width), BF16),
             pltpu.VMEM((side, tile, tile, width), BF16),
-            pltpu.VMEM((side, tile, tile, width), BF16),
+            pltpu.VMEM((2, tile, tile, width), BF16),
+            pltpu.VMEM((tile, tile, width), BF16),
             pltpu.VMEM((tile, tile, width), F32),
             pltpu.VMEM((tile, tile, width), F32),
             pltpu.VMEM((tile, tile, width), F32),
@@ -541,36 +721,34 @@
             pltpu.VMEM((cells, 4 * width), BF16),
             pltpu.VMEM((width, width), F32),
             pltpu.VMEM((4 * width, width), F32),
-            pltpu.VMEM((team, piece, width), BF16),
-            pltpu.VMEM((team, piece, width), BF16),
-            pltpu.VMEM((team, piece, width), BF16),
+            pltpu.VMEM((2, team, piece, width), BF16),
+            pltpu.VMEM((2, team, piece, width), BF16),
+            pltpu.VMEM((2, team, piece, width), BF16),
+            dma((11,)),
+            dma((side + 1, 2)),
+            dma((side, 2)),
             dma((side,)),
             dma((side,)),
-            dma((side,)),
-            dma((side,)),
-            dma((side,)),
-            dma((side,)),
-            dma((team,)),
-            dma((team,)),
-            dma((team,)),
-            dma((team,)),
+            dma((side, 2)),
+            dma((2, 2)),
+            dma((2,)),
+            dma((2, team)),
+            dma((2, team)),
+            dma((2, team)),
+            dma((2, team)),
         ],
         compiler_params=pltpu.CompilerParams(
-            collective_id=0, has_side_effects=True, vmem_limit_bytes=40 * 1024 * 1024
+            collective_id=0, has_side_effects=True, vmem_limit_bytes=64 * 1024 * 1024
         ),
-    )(
-        pair_norm.reshape(cells, width),
-        pair_rstd,
-        out_norm.reshape(cells, width),
-        out_rstd,
-        grad_out.reshape(cells, width),
-        mask,
-        proj_weight,
-        gate_weight,
-        out_weight,
-        out_gain.reshape(1, width),
-        out_bias.reshape(1, width),
-    )
+    )(*arrays)
+    pair_grad, proj_wgrad, gate_wgrad = pl.pallas_call(
+        flush,
+        out_shape=shapes,
+        in_specs=[hbm] * 3,
+        out_specs=(hbm, hbm, hbm),
+        scratch_shapes=[pltpu.VMEM(a.shape, a.dtype) for a in shapes] + [dma((2, 3))],
+        compiler_params=pltpu.CompilerParams(vmem_limit_bytes=64 * 1024 * 1024),
+    )(*made)
     return pair_grad.reshape(tile, tile, width), proj_wgrad, gate_wgrad
 
 
@@ -580,15 +758,12 @@
     hidden = rest[7].shape[0]
     team = rows * cols
     fits = (
-        rows == cols
+        rows == cols == 4
         and tile_rows == tile_cols
         and tile_rows % 16 == 0
         and tile_rows <= 32
         and hidden == width
         and width == 128
-        and 8 <= team <= 32
-        and width % team == 0
-        and 4 * width // team % 16 == 0
     )
     return (fused if fits else plain)(pair_norm, *rest)
 

time: 67.4 us -> 56.1 us (0.83)
  local copies, waits for them, and re-layouts: 8.72 us -> 0 us
  Pallas kernels: 57.6 us -> 55.3 us
    unnamed x25 -> x0, local copies, waits for them, and re-layouts: 8.65 us -> none
    pallas_call x1 -> x2, Pallas kernels: 57.6 us -> 55.3 us  [the longest x1 53.3 us: fused(): pl.pallas_call(functools.partial(kernel, side, tile), out_shape=shapes, i...]
where the time goes in v2:
time: 56.1 us; the launch traced here: 56 us
  Pallas kernels  55.3 us (99%)
  between operations  0.64 us (1%)
    pallas_call x1, Pallas kernels, fused(): pl.pallas_call(functools.partial(kernel, side, tile), out_shape=shapes, i...  53.3 us
    pallas_call x1, Pallas kernels, fused(): pl.pallas_call(flush, out_shape=shapes, in_specs=[hbm] * 3, out_specs=(hb...  1.98 us

profile of v2, /device:TPU:0, one launch (start us, length us, event | category | flops | bytes accessed | tf_op | source)
XLA Modules:
  0.0 56.0 jit_solution(3076900469965186636)
XLA Ops:
  0.6 53.3 %shard_map.130 = (f32[1024,128]{1,0:T(8,128)}, f32[128,512]{1,0:T(8,128)}, f32[128,128]{1,0:T(8,128)}) custom-call(bf16[1024,128]{1,0:T(8,128)(2,1)} %bitcast.7, f32[32,32]{1,0:T(8,128)} %pair_rstd_hbm.1, bf16[1024,128]{1,0:T(8,128)(2,1)} %bitcast.8, f32[32,32]{1,0:T(8,128)} %out_rstd_hbm.1, bf16[1024,128]{1,0:T(8,128)(2,1)} %bitcast.9, s32[1,128]{1,0:T(1,128)} %bitcast.10, ...), custom_call_target="tpu_custom_call" | custom-call | tf_op jit(solution)/shard_map/pallas_call | solution.py:699
  54.0 2.0 %shard_map.131 = (f32[1024,128]{1,0:T(8,128)}, f32[128,512]{1,0:T(8,128)}, f32[128,128]{1,0:T(8,128)}) custom-call(f32[1024,128]{1,0:T(8,128)} %get-tuple-element.9.refs_0_, f32[128,512]{1,0:T(8,128)} %get-tuple-element.10.refs_1_, f32[128,128]{1,0:T(8,128)} %get-tuple-element.11.refs_2_), custom_call_target="tpu_custom_call" | custom-call | tf_op jit(solution)/shard_map/pallas_call | solution.py:744

commit v3 on v2

--- a/solution.py
+++ b/solution.py
@@ -179,6 +179,10 @@
     w_out,
     w_in,
     w_all,
+    g_out,
+    g_in,
+    g_all,
+    gate32,
     load_sem,
     tri_send,
     tri_recv,
@@ -294,17 +298,18 @@
 
     def w_copy(k, peer, source):
         return remote(
-            w_out.at[k, peer],
-            w_in.at[k, source],
+            g_out.at[peer] if k == 2 else w_out.at[k, peer],
+            g_in.at[source] if k == 2 else w_in.at[k, source],
             w_send.at[k, peer],
             w_recv.at[k, source],
             place(peer),
         )
 
     def all_copy(k, peer, source):
+        held = g_all.at[source] if k == 2 else w_all.at[k, source]
         return remote(
-            w_all.at[k, source],
-            w_all.at[k, source],
+            held,
+            held,
             all_send.at[k, peer],
             all_recv.at[k, source],
             place(peer),
@@ -312,56 +317,67 @@
 
     gate_acc[...] = jnp.zeros_like(gate_acc)
     proj_acc[...] = jnp.zeros_like(proj_acc)
+    upper = col // 2
+    inner = lax.rem(col + upper, 2)
+
+    def mirror(t):
+        return t + upper * (3 - 2 * t)
+
+    def block_at(s):
+        return mirror(s if s >= 2 else inner + s * (1 - 2 * inner))
+
+    toward_end, toward_middle = mirror(0), mirror(inner + 1)
+
     for load in loads[:8]:
         load.wait()
 
-    def first(n, carry):
-        here = spot(n)
-        x = x_ref[here, :]
-        gate = jax.nn.sigmoid(jnp.dot(x, gate_ref[...], preferred_element_type=F32))
-        hat = hat_ref[here, :].astype(F32)
-        y = (hat * gain_ref[...] + bias_ref[...]).astype(BF16)
-        update = jnp.dot(y, out_ref[...], preferred_element_type=F32)
-        up = up_ref[here, :].astype(F32)
-        grad = (up * update * gate * (1.0 - gate)).astype(BF16)
-        gate_grad[here, :] = grad
-        dy = (
-            lax.dot_general(
-                (up * gate).astype(BF16), out_ref[...], LANES_DOT, preferred_element_type=F32
+    def first(h):
+        span = pl.ds(h * part, part)
+
+        def body(n, carry):
+            rows = 2 * step_rows
+            lines = pl.ds(pl.multiple_of(n * rows, rows), rows)
+            gate = jax.nn.sigmoid(
+                jnp.dot(
+                    x_ref[lines, span, :].reshape(cells, width),
+                    gate_ref[...],
+                    preferred_element_type=F32,
+                )
             )
-            * gain_ref[...]
-        )
-        tri = spread_cells(out_rstd_ref, n) * (
-            dy
-            - jnp.mean(dy, axis=-1, keepdims=True)
-            - hat * jnp.mean(dy * hat, axis=-1, keepdims=True)
-        )
-        tri_all[col, lead(n)] = tri.astype(BF16).reshape(step_rows, tile, width)
-        return carry
-
-    lax.fori_loop(0, chunks, first, 0)
-    for load in loads[8:]:
-        load.wait()
-    pl.semaphore_wait(barrier, team - 1)
-
-    upper = col // 2
-    inner = lax.rem(col + upper, 2)
-
-    def mirror(t):
-        return t + upper * (3 - 2 * t)
-
-    def block_at(s):
-        return mirror(s if s >= 2 else inner + s * (1 - 2 * inner))
-
-    toward_end, toward_middle = mirror(0), mirror(inner + 1)
+            gate32[lines, span, :] = gate.reshape(rows, part, width)
+            hat = hat_ref[lines, span, :].reshape(cells, width).astype(F32)
+            up = up_ref[lines, span, :].reshape(cells, width).astype(F32)
+            dy = (
+                lax.dot_general(
+                    (up * gate).astype(BF16), out_ref[...], LANES_DOT, preferred_element_type=F32
+                )
+                * gain_ref[...]
+            )
+            rstd = out_rstd_ref[lines, :][:, h * part : (h + 1) * part]
+            rstd = jnp.broadcast_to(rstd[:, :, None], (rows, part, width)).reshape(cells, width)
+            tri = rstd * (
+                dy
+                - jnp.mean(dy, axis=-1, keepdims=True)
+                - hat * jnp.mean(dy * hat, axis=-1, keepdims=True)
+            )
+            tri_all[col, lines, span, :] = tri.astype(BF16).reshape(rows, part, width)
+            return carry
+
+        lax.fori_loop(0, tile // (2 * step_rows), body, 0)
 
     for h in range(2):
+        first(h)
+        if h == 0:
+            pl.semaphore_wait(barrier, team - 1)
         tri_copy(col, h, 0, toward_middle).start()
 
         @pl.when(inner == 1)
         def _(h=h):
             tri_copy(col, h, 1, toward_end).start()
 
+    for load in loads[8:]:
+        load.wait()
+
     def forward_to(s):
         return toward_middle if s == 1 else toward_end
 
@@ -380,7 +396,7 @@
 
     def second(n, carry):
         here = spot(n)
-        proj = jnp.dot(x_ref[here, :], proj_ref[...], preferred_element_type=F32)
+        proj = jnp.dot(x_ref[lead(n)].reshape(cells, width), proj_ref[...], preferred_element_type=F32)
         at = pl.multiple_of(row * tile + n * step_rows, step_rows)
         row_mask = mask_ref[pl.ds(at, step_rows), :]
         mask = (row_mask[:, None, :] * col_mask[None, :, :]).reshape(cells, width)
@@ -461,13 +477,60 @@
 
         lax.fori_loop(0, tile // GROUP, body, 0)
 
+    piece = 2 * width // team
+    gate_piece = width // team
+
+    def send_pieces(k):
+        if k == 2:
+            g_out[...] = gate_acc[...].reshape(team, gate_piece, width)
+        else:
+            half = proj_acc[2 * k * width : 2 * (k + 1) * width, :]
+            w_out[k] = half.reshape(team, piece, width).astype(BF16)
+
+        def body(off, carry):
+            w_copy(k, lax.rem(me + off, team), me).start()
+            return carry
+
+        lax.fori_loop(1, team, body, 0)
+        if k == 2:
+            g_in[me] = g_out[me]
+        else:
+            w_in[k, me] = w_out[k, me]
+
+    def send_totals(k):
+        def body(off, carry):
+            w_copy(k, me, lax.rem(me + off, team)).wait_recv()
+            return carry
+
+        lax.fori_loop(1, team, body, 0)
+        parts = g_in if k == 2 else w_in.at[k]
+        total = parts[0].astype(F32)
+        for p in range(1, team):
+            total = total + parts[p].astype(F32)
+        if k == 2:
+            g_all[me] = total
+        else:
+            w_all[k, me] = total.astype(BF16)
+
+        def push(off, carry):
+            all_copy(k, lax.rem(me + off, team), me).start()
+            return carry
+
+        lax.fori_loop(1, team, push, 0)
+
     for h in range(2):
         do_part(0, h)
 
     def third(n, carry):
         here = spot(n)
+        gate = gate32[lead(n)].reshape(cells, width)
+        hat = hat_ref[lead(n)].reshape(cells, width).astype(F32)
+        y = (hat * gain_ref[...] + bias_ref[...]).astype(BF16)
+        update = jnp.dot(y, out_ref[...], preferred_element_type=F32)
+        up = up_ref[lead(n)].reshape(cells, width).astype(F32)
+        gate_grad[here, :] = (up * update * gate * (1.0 - gate)).astype(BF16)
         gate_acc[...] += lax.dot_general(
-            x_ref[here, :], gate_grad[here, :], ROWS_DOT, preferred_element_type=F32
+            x_ref[lead(n)].reshape(cells, width), gate_grad[here, :], ROWS_DOT, preferred_element_type=F32
         )
         return carry
 
@@ -491,11 +554,12 @@
         for h in range(2):
             do_relay(s, h)
         if s == side - 1:
+            send_pieces(2)
             do_left(s)
 
     def weights(n, grads, base):
         here = spot(n)
-        x = x_ref[here, :]
+        x = x_ref[lead(n)].reshape(cells, width)
         for q, grad in enumerate(grads):
             grad = grad.astype(BF16)
             at = (base + q) * width
@@ -519,47 +583,9 @@
         weights(n, (grad * right_a[here, :], grad * right_b[here, :]), 2)
         return carry
 
-    piece = 2 * width // team
-    gate_piece = width // team
-
-    def send_pieces(k):
-        half = proj_acc[2 * k * width : 2 * (k + 1) * width, :]
-        w_out[k, :, 0:piece, :] = half.reshape(team, piece, width).astype(BF16)
-
-        def body(off, carry):
-            w_copy(k, lax.rem(me + off, team), me).start()
-            return carry
-
-        lax.fori_loop(1, team, body, 0)
-        w_in[k, me] = w_out[k, me]
-
-    def send_totals(k):
-        def body(off, carry):
-            w_copy(k, me, lax.rem(me + off, team)).wait_recv()
-            return carry
-
-        lax.fori_loop(1, team, body, 0)
-        total = w_in[k, 0].astype(F32)
-        for p in range(1, team):
-            total = total + w_in[k, p].astype(F32)
-        w_all[k, me] = total.astype(BF16)
-
-        def push(off, carry):
-            all_copy(k, lax.rem(me + off, team), me).start()
-            return carry
-
-        lax.fori_loop(1, team, push, 0)
-
     lax.fori_loop(0, chunks, left_weights, 0)
-    w_out[0, :, piece : piece + 16, :] = jnp.concatenate(
-        [
-            gate_acc[...].reshape(team, gate_piece, width),
-            jnp.zeros((team, 16 - gate_piece, width), F32),
-        ],
-        axis=1,
-    ).astype(BF16)
-    w_out[1, :, piece : piece + 16, :] = jnp.zeros((team, 16, width), BF16)
     send_pieces(0)
+    send_totals(2)
     for kind in range(2):
         for h in range(2):
             part_copy(row, h, kind, sibling).wait_recv()
@@ -574,7 +600,7 @@
         ) + lax.dot_general(
             proj_grad[here, :], proj_ref[...], LANES_DOT, preferred_element_type=F32
         )
-        x = x_ref[here, :].astype(F32)
+        x = x_ref[lead(n)].reshape(cells, width).astype(F32)
         pair_out[here, :] = spread_cells(pair_rstd_ref, n) * (
             grad
             - jnp.mean(grad, axis=-1, keepdims=True)
@@ -604,7 +630,7 @@
 
     def finish(off, carry):
         peer = lax.rem(me + off, team)
-        for k in range(2):
+        for k in range(3):
             w_copy(k, peer, me).wait_send()
         return carry
 
@@ -612,7 +638,7 @@
 
     def get_totals(off, carry):
         peer = lax.rem(me + off, team)
-        for k in range(2):
+        for k in range(3):
             all_copy(k, me, peer).wait_recv()
         return carry
 
@@ -620,7 +646,7 @@
 
     def finish_totals(off, carry):
         peer = lax.rem(me + off, team)
-        for k in range(2):
+        for k in range(3):
             all_copy(k, peer, me).wait_send()
         return carry
 
@@ -630,11 +656,9 @@
     for q in range(4):
         k, at = q // 2, (q % 2) * each
         proj_out[:, q * width : (q + 1) * width] = (
-            w_all[k, at : at + each, 0:piece, :].astype(F32).reshape(width, width)
-        )
-    gate_out[...] = (
-        w_all[0, :, piece : piece + 16, :].astype(F32)[:, 0:gate_piece, :].reshape(width, width)
-    )
+            w_all[k, at : at + each].astype(F32).reshape(width, width)
+        )
+    gate_out[...] = g_all[...].reshape(width, width)
 
 
 def flush(*refs):
@@ -673,7 +697,7 @@
     side = lax.axis_size("row")
     team = side * side
     cells = tile * tile
-    piece = 2 * width // team + 16
+    piece = 2 * width // team
     tokens = token_mask.shape[0]
     vmem = pl.BlockSpec(memory_space=pltpu.VMEM)
     hbm = pl.BlockSpec(memory_space=pltpu.HBM)
@@ -684,11 +708,11 @@
         jax.ShapeDtypeStruct((width, width), F32),
     )
     arrays = (
-        pair_norm.reshape(cells, width),
+        pair_norm,
         pair_rstd,
-        out_norm.reshape(cells, width),
+        out_norm,
         out_rstd,
-        grad_out.reshape(cells, width),
+        grad_out,
         token_mask.reshape(1, tokens),
         proj_weight,
         gate_weight,
@@ -724,6 +748,10 @@
             pltpu.VMEM((2, team, piece, width), BF16),
             pltpu.VMEM((2, team, piece, width), BF16),
             pltpu.VMEM((2, team, piece, width), BF16),
+            pltpu.VMEM((team, width // team, width), F32),
+            pltpu.VMEM((team, width // team, width), F32),
+            pltpu.VMEM((team, width // team, width), F32),
+            pltpu.VMEM((tile, tile, width), F32),
             dma((11,)),
             dma((side + 1, 2)),
             dma((side, 2)),
@@ -732,10 +760,10 @@
             dma((side, 2)),
             dma((2, 2)),
             dma((2,)),
-            dma((2, team)),
-            dma((2, team)),
-            dma((2, team)),
-            dma((2, team)),
+            dma((3, team)),
+            dma((3, team)),
+            dma((3, team)),
+            dma((3, team)),
         ],
         compiler_params=pltpu.CompilerParams(
             collective_id=0, has_side_effects=True, vmem_limit_bytes=64 * 1024 * 1024

time: 56.1 us -> 56.1 us (level)
  no operation moved by 1% of the time
where the time goes in v3:
time: 56.1 us; the launch traced here: 56 us
  Pallas kernels  55.3 us (99%)
  between operations  0.64 us (1%)
    pallas_call x1, Pallas kernels, fused(): pl.pallas_call(functools.partial(kernel, side, tile), out_shape=shapes, i...  53.4 us
    pallas_call x1, Pallas kernels, fused(): pl.pallas_call(flush, out_shape=shapes, in_specs=[hbm] * 3, out_specs=(hb...  1.98 us

profile of v3, /device:TPU:0, one launch (start us, length us, event | category | flops | bytes accessed | tf_op | source)
XLA Modules:
  0.0 56.0 jit_solution(2651525491238199309)
XLA Ops:
  0.6 53.4 %shard_map.130 = (f32[1024,128]{1,0:T(8,128)}, f32[128,512]{1,0:T(8,128)}, f32[128,128]{1,0:T(8,128)}) custom-call(bf16[32,32,128]{2,1,0:T(8,128)(2,1)} %x_hbm.1, f32[32,32]{1,0:T(8,128)} %pair_rstd_hbm.1, bf16[32,32,128]{2,1,0:T(8,128)(2,1)} %hat_hbm.1, f32[32,32]{1,0:T(8,128)} %out_rstd_hbm.1, bf16[32,32,128]{2,1,0:T(8,128)(2,1)} %up_hbm.1, ...), custom_call_target="tpu_custom_call" | custom-call | tf_op jit(solution)/shard_map/pallas_call | solution.py:723
  54.0 2.0 %shard_map.131 = (f32[1024,128]{1,0:T(8,128)}, f32[128,512]{1,0:T(8,128)}, f32[128,128]{1,0:T(8,128)}) custom-call(f32[1024,128]{1,0:T(8,128)} %get-tuple-element.9.refs_0_, f32[128,512]{1,0:T(8,128)} %get-tuple-element.10.refs_1_, f32[128,128]{1,0:T(8,128)} %get-tuple-element.11.refs_2_), custom_call_target="tpu_custom_call" | custom-call | tf_op jit(solution)/shard_map/pallas_call | solution.py:772

commit v4 on v3

--- a/solution.py
+++ b/solution.py
@@ -178,6 +178,7 @@
     proj_acc,
     w_out,
     w_in,
+    c_all,
     w_all,
     g_out,
     g_in,
@@ -480,6 +481,31 @@
     piece = 2 * width // team
     gate_piece = width // team
 
+    def quarter_copy(q, source):
+        return remote(
+            w_out.at[q], w_in.at[source], w_send.at[0, q], w_recv.at[0, source], {"row": q}
+        )
+
+    def col_copy(peer, source):
+        held = c_all.at[source]
+        return remote(held, held, w_send.at[1, peer], w_recv.at[1, source], {"col": peer})
+
+    def row_copy(peer, source):
+        held = w_all.at[source]
+        return remote(held, held, all_send.at[0, peer], all_recv.at[0, source], {"row": peer})
+
+    def send_quarters(start):
+        for q in range(start, start + 2):
+            w_out[q] = proj_acc[q * width : (q + 1) * width, :].astype(BF16)
+
+            @pl.when(row != q)
+            def _(q=q):
+                quarter_copy(q, row).start()
+
+            @pl.when(row == q)
+            def _(q=q):
+                w_in[row] = w_out[q]
+
     def send_pieces(k):
         if k == 2:
             g_out[...] = gate_acc[...].reshape(team, gate_piece, width)
@@ -584,14 +610,13 @@
         return carry
 
     lax.fori_loop(0, chunks, left_weights, 0)
-    send_pieces(0)
+    send_quarters(0)
     send_totals(2)
     for kind in range(2):
         for h in range(2):
             part_copy(row, h, kind, sibling).wait_recv()
     lax.fori_loop(0, chunks, right_weights, 0)
-    send_pieces(1)
-    send_totals(0)
+    send_quarters(2)
 
     def last(n, carry):
         here = spot(n)
@@ -608,9 +633,30 @@
         )
         return carry
 
-    lax.fori_loop(0, chunks // 2, last, 0)
-    send_totals(1)
-    lax.fori_loop(chunks // 2, chunks, last, 0)
+    lax.fori_loop(0, 1, last, 0)
+    for r in range(1, side):
+        quarter_copy(row, lax.rem(row + r, side)).wait_recv()
+    total = w_in[0].astype(F32)
+    for r in range(1, side):
+        total = total + w_in[r].astype(F32)
+    c_all[col] = total.astype(BF16)
+    for r in range(1, side):
+        col_copy(lax.rem(col + r, side), col).start()
+    lax.fori_loop(1, 3, last, 0)
+    for r in range(1, side):
+        col_copy(col, lax.rem(col + r, side)).wait_recv()
+    total = c_all[0].astype(F32)
+    for r in range(1, side):
+        total = total + c_all[r].astype(F32)
+    w_all[row] = total.astype(BF16)
+    for r in range(1, side):
+        row_copy(lax.rem(row + r, side), row).start()
+    lax.fori_loop(3, chunks, last, 0)
+    for r in range(1, side):
+        quarter_copy(lax.rem(row + r, side), row).wait_send()
+        col_copy(lax.rem(col + r, side), col).wait_send()
+        row_copy(lax.rem(row + r, side), row).wait_send()
+        row_copy(row, lax.rem(row + r, side)).wait_recv()
 
     for h in range(2):
         tri_copy(col, h, 0, toward_middle).wait_send()
@@ -630,7 +676,7 @@
 
     def finish(off, carry):
         peer = lax.rem(me + off, team)
-        for k in range(3):
+        for k in range(2, 3):
             w_copy(k, peer, me).wait_send()
         return carry
 
@@ -638,7 +684,7 @@
 
     def get_totals(off, carry):
         peer = lax.rem(me + off, team)
-        for k in range(3):
+        for k in range(2, 3):
             all_copy(k, me, peer).wait_recv()
         return carry
 
@@ -646,18 +692,14 @@
 
     def finish_totals(off, carry):
         peer = lax.rem(me + off, team)
-        for k in range(3):
+        for k in range(2, 3):
             all_copy(k, peer, me).wait_send()
         return carry
 
     lax.fori_loop(1, team, finish_totals, 0)
 
-    each = width // piece
     for q in range(4):
-        k, at = q // 2, (q % 2) * each
-        proj_out[:, q * width : (q + 1) * width] = (
-            w_all[k, at : at + each].astype(F32).reshape(width, width)
-        )
+        proj_out[:, q * width : (q + 1) * width] = w_all[q].astype(F32)
     gate_out[...] = g_all[...].reshape(width, width)
 
 
@@ -745,9 +787,10 @@
             pltpu.VMEM((cells, 4 * width), BF16),
             pltpu.VMEM((width, width), F32),
             pltpu.VMEM((4 * width, width), F32),
-            pltpu.VMEM((2, team, piece, width), BF16),
-            pltpu.VMEM((2, team, piece, width), BF16),
-            pltpu.VMEM((2, team, piece, width), BF16),
+            pltpu.VMEM((4, width, width), BF16),
+            pltpu.VMEM((4, width, width), BF16),
+            pltpu.VMEM((4, width, width), BF16),
+            pltpu.VMEM((4, width, width), BF16),
             pltpu.VMEM((team, width // team, width), F32),
             pltpu.VMEM((team, width // team, width), F32),
             pltpu.VMEM((team, width // team, width), F32),

time: 56.1 us -> 58.7 us (1.046)
  Pallas kernels: 55.3 us -> 57.9 us
    pallas_call x1, Pallas kernels: 53.4 us -> 55.9 us  [fused(): pl.pallas_call(functools.partial(kernel, side, tile), out_shape=shapes, i...]
where the time goes in v4:
time: 58.7 us; the launch traced here: 58.5 us
  Pallas kernels  57.9 us (99%)
  between operations  0.64 us (1%)
    pallas_call x1, Pallas kernels, fused(): pl.pallas_call(functools.partial(kernel, side, tile), out_shape=shapes, i...  55.9 us
    pallas_call x1, Pallas kernels, fused(): pl.pallas_call(flush, out_shape=shapes, in_specs=[hbm] * 3, out_specs=(hb...  1.98 us

profile of v4, /device:TPU:0, one launch (start us, length us, event | category | flops | bytes accessed | tf_op | source)
XLA Modules:
  0.0 58.5 jit_solution(5656403479873905469)
XLA Ops:
  0.6 55.9 %shard_map.130 = (f32[1024,128]{1,0:T(8,128)}, f32[128,512]{1,0:T(8,128)}, f32[128,128]{1,0:T(8,128)}) custom-call(bf16[32,32,128]{2,1,0:T(8,128)(2,1)} %x_hbm.1, f32[32,32]{1,0:T(8,128)} %pair_rstd_hbm.1, bf16[32,32,128]{2,1,0:T(8,128)(2,1)} %hat_hbm.1, f32[32,32]{1,0:T(8,128)} %out_rstd_hbm.1, bf16[32,32,128]{2,1,0:T(8,128)(2,1)} %up_hbm.1, ...), custom_call_target="tpu_custom_call" | custom-call | tf_op jit(solution)/shard_map/pallas_call | solution.py:765
  56.5 2.0 %shard_map.131 = (f32[1024,128]{1,0:T(8,128)}, f32[128,512]{1,0:T(8,128)}, f32[128,128]{1,0:T(8,128)}) custom-call(f32[1024,128]{1,0:T(8,128)} %get-tuple-element.9.refs_0_, f32[128,512]{1,0:T(8,128)} %get-tuple-element.10.refs_1_, f32[128,128]{1,0:T(8,128)} %get-tuple-element.11.refs_2_), custom_call_target="tpu_custom_call" | custom-call | tf_op jit(solution)/shard_map/pallas_call | solution.py:815
